TPU v7x, 32 devices: a whole 2x2x4 slice. The times are simulated.
32 devices in a mesh: ctx: 8 (over y, x, core), head: 4 (over z).
Axes of the slice: x: 2, y: 2, z: 4, core: 2. Of those that a mesh axis runs over, the one named last changes fastest.
Arguments:
- activations: bfloat16 [4096, 4096], P('ctx')
- qkv_weight: bfloat16 [4096, 3, 32, 128], P(None, None, 'head'), may hold values from -0.09375 to 0.09375
- out_weight: bfloat16 [32, 128, 4096], P('head'), may hold values from -0.09375 to 0.09375
- mod_table: float32 [16, 4096], replicated, may hold values from -3 to 3
- clip_level: int32 [32], replicated, may hold values from 0 to 15
- clip_of: int32 [4096], P('ctx'), may hold values from 0 to 31, never falling along the last dimension, each value on 1 to 256 neighbouring positions
- visible: int32 [32, 32], replicated, may hold values from 0 to 1, as said below
Outputs:
- mixed: bfloat16 [4096, 4096], P(('ctx', 'head'))
Inputs may be any that keep to these rules, and one draw needn't show every extreme that they name: visible is 1 on the diagonal and 0 above it. `clip_of`: clip numbers never fall along the tokens; every clip has 1 to 256 tokens and one has exactly 256.
All inputs are finite; a program needn't handle non-finite values.
Results may differ from a plain program's by a relative error of at most 0.02.
The roundings to bfloat16 on the way count: a program that leaves them out, or rounds other values in their place, can miss the bound.
Values may be sent and summed in bfloat16 or wider, within the bound.
A program may use at most 128 MiB of HBM per device.

v0:
```python
import math

import jax
import jax.numpy as jnp
from jax import lax
from jax.sharding import PartitionSpec as P


def score_block(state_now, kv_block, key_clips, queries, query_vis, score_scale):
    clip_count = query_vis.shape[1]
    clip_ids = lax.broadcasted_iota(jnp.int32, (1, clip_count), 1)
    key_hot = (key_clips[:, None] == clip_ids).astype(jnp.float32)
    allowed = jnp.dot(query_vis, key_hot.T, precision=lax.Precision.HIGHEST) > 0.5
    top_score, totals, summed = state_now
    key_rows = kv_block[:, 0]
    value_rows = kv_block[:, 1]
    scores = (
        jnp.einsum("rhd,khd->hrk", queries, key_rows, preferred_element_type=jnp.float32)
        * score_scale
    )
    masked = jnp.where(allowed[None], scores, -1e30)
    new_top = jnp.maximum(top_score, jnp.max(masked, axis=2))
    weights = jnp.where(allowed[None], jnp.exp(masked - new_top[:, :, None]), 0.0)
    factor = jnp.exp(top_score - new_top)
    totals = totals * factor + jnp.sum(weights, axis=2)
    summed = summed * factor[:, :, None] + jnp.einsum(
        "hrk,khd->hrd", weights.astype(jnp.bfloat16), value_rows, preferred_element_type=jnp.float32
    )
    return (new_top, totals, summed)


def fold_keys(state_now, kv_rows, key_clips, queries, query_vis, score_scale):
    key_count = kv_rows.shape[0]
    block_rows = math.gcd(key_count, 512)

    def one_block(block_index, state_in):
        first_row = block_index * block_rows
        kv_block = lax.dynamic_slice_in_dim(kv_rows, first_row, block_rows, 0)
        clip_block = lax.dynamic_slice_in_dim(key_clips, first_row, block_rows, 0)
        return score_block(state_in, kv_block, clip_block, queries, query_vis, score_scale)

    return lax.fori_loop(0, key_count // block_rows, one_block, state_now)


def per_device(activations, qkv_weight, out_weight, mod_table, clip_level, clip_of, visible):
    heads_here = qkv_weight.shape[2]
    head_size = qkv_weight.shape[3]
    clip_count = visible.shape[0]
    level_count = mod_table.shape[0]
    clip_ids = lax.broadcasted_iota(jnp.int32, (1, clip_count), 1)
    level_ids = lax.broadcasted_iota(jnp.int32, (1, level_count), 1)
    tok_hot = clip_of[:, None] == clip_ids
    level_rows = jnp.sum(jnp.where(tok_hot, clip_level[None, :], 0), axis=1)
    level_hot = (level_rows[:, None] == level_ids).astype(jnp.float32)
    modulation = jnp.dot(level_hot, mod_table, precision=lax.Precision.HIGHEST)
    moduled = (activations.astype(jnp.float32) * (1.0 + modulation)).astype(jnp.bfloat16)
    qkv = jnp.einsum(
        "td,dchk->tchk", moduled, qkv_weight, preferred_element_type=jnp.float32
    ).astype(jnp.bfloat16)
    queries = qkv[:, 0]
    kv_local = qkv[:, 1:3]
    query_count = queries.shape[0]
    query_hot = (clip_of[:, None] == clip_ids).astype(jnp.float32)
    query_vis = jnp.dot(query_hot, visible.astype(jnp.float32), precision=lax.Precision.HIGHEST)
    score_scale = 1.0 / jnp.sqrt(jnp.float32(head_size))
    initial = (
        jnp.full((heads_here, query_count), -1e30, jnp.float32),
        jnp.zeros((heads_here, query_count), jnp.float32),
        jnp.zeros((heads_here, query_count, head_size), jnp.float32),
    )
    kv_all, clips_all = (
        lax.all_gather(kv_local, "ctx", axis=0, tiled=True),
        lax.all_gather(clip_of, "ctx", axis=0, tiled=True),
    )
    final = fold_keys(initial, kv_all, clips_all, queries, query_vis, score_scale)
    attended = (final[2] / final[1][:, :, None]).astype(jnp.bfloat16)
    attended_rows = jnp.transpose(attended, (1, 0, 2))
    return lax.psum_scatter(
        jnp.einsum(
            "rhd,hdo->ro", attended_rows, out_weight, preferred_element_type=jnp.float32
        ).astype(jnp.bfloat16),
        "head",
        scatter_dimension=0,
        tiled=True,
    )


def solution(mesh):
    placed = (
        P("ctx", None),
        P(None, None, "head", None),
        P("head", None, None),
        P(),
        P(),
        P("ctx"),
        P(),
    )
    return jax.shard_map(
        per_device, mesh=mesh, in_specs=placed, out_specs=P(("ctx", "head"), None), check_vma=False
    )
```

profile of v0, /device:TPU:14, one launch (start us, length us, event | category | flops | bytes accessed | tf_op | source)
XLA Modules:
  0.0 310.9 jit_solution(3600306617005827041)
XLA Ops:
  7.5 5.6 %fusion.20 = bf16[512,4096,1,1]{1,0,3,2:T(8,128)(2,1)S(1)} fusion(f32[16,4096]{1,0:T(8,128)S(1)} %copy-done, bf16[512,4096]{1,0:T(8,128)(2,1)} %param.9, s32[512]{0:T(512)S(1)} %select_reduce_fusion), kind=kOutput, calls=%fused_computation.29 | convolution fusion | flops 411049984 | bytes 8652800 | tf_op jit(solution)/shard_map/dot_general | solution.py:55
  13.1 17.1 %fusion.21 = bf16[512,3,8,128]{3,0,2,1:T(8,128)(2,1)S(1)} fusion(bf16[512,4096,1,1]{1,0,3,2:T(8,128)(2,1)S(1)} %fusion.20, bf16[4096,3,8,128]{3,2,1,0:T(8,128)(2,1)} %param.10), kind=kOutput, calls=%fused_computation.30 | convolution fusion | flops 12886474752 | bytes 32505856 | tf_op jit(solution)/shard_map/td,dchk->tchk/dot_general | solution.py:57
  33.5 8.1 %all-gather = s32[8,1,512]{2,1,0:T(1,128)S(1)} all-gather(s32[1,1,512]{2,1,0:T(1,128)S(1)} %bitcast.58), channel_id=1, replica_groups=mesh['ctx'=8,'head'=4] {'ctx'}, dimensions={0}, use_global_device_ids=true | all-gather | bytes 18432 | tf_op jit(solution)/shard_map/all_gather | solution.py:73
  43.5 80.1 %all-gather.3.cloned.1.call-done = bf16[4096,2,8,128]{3,0,2,1:T(8,128)(2,1)} async-done(((bf16[512,2,8,128]{3,0,2,1:T(8,128)(2,1)}), bf16[4096,2,8,128]{3,0,2,1:T(8,128)(2,1)}) %all-gather.3.cloned.1.call-update) | async-done | bytes 16777232 | tf_op jit(solution)/shard_map/all_gather | solution.py:72
  123.6 93.5 %while.18 = (s32[]{:T(128)}, f32[8,512]{1,0:T(8,128)S(1)}, f32[8,512]{1,0:T(8,128)S(1)}, f32[8,512,128]{2,1,0:T(8,128)}, s32[4096]{0:T(1024)S(1)}, /*index=5*/f3...) while((s32[]{:T(128)}, f32[8,512]{1,0:T(8,128)S(1)}, ...), condition=%wide.region_4.5_spmd.clone, body=%wide.region_1.4_spmd.clone.sunk | while | flops 1203539968 | bytes 50665744 | solution.py:42
  124.3 2.9 fusion.46
  129.3 4.6 %fusion.49 = f32[8,512,128]{2,1,0:T(8,128)S(1)} fusion(f32[8,512,128]{2,1,0:T(8,128)S(1)} %copy-done.5, f32[8,512,512]{2,1,0:T(8,128)S(1)} %get-tuple-element.272, f32[8,512]{1,0:T(8,128)S(1)} %select_maximum_fusion.2, pred[512,512]{0,1:T(8,128)(4,1)S(1)} %fusion.45, bf16[4096,2,8,128]{3,0,2,1:T(8,128)(2,1)} %get-tuple-element.307, ...), kind=kOutput, calls=%fused_computation.8.clone.1 | convolution fusion | flops 548929536 | bytes 13926409 | tf_op jit(solution)/shard_map/while/body/eval_jaxpr/hrk,khd->hrd/dot_general | solution.py:26
  136.0 2.9 fusion.46
  141.0 4.6 %fusion.49 = f32[8,512,128]{2,1,0:T(8,128)S(1)} fusion(f32[8,512,128]{2,1,0:T(8,128)S(1)} %copy-done.5, f32[8,512,512]{2,1,0:T(8,128)S(1)} %get-tuple-element.272, f32[8,512]{1,0:T(8,128)S(1)} %select_maximum_fusion.2, pred[512,512]{0,1:T(8,128)(4,1)S(1)} %fusion.45, bf16[4096,2,8,128]{3,0,2,1:T(8,128)(2,1)} %get-tuple-element.307, ...), kind=kOutput, calls=%fused_computation.8.clone.1 | convolution fusion | flops 548929536 | bytes 13926409 | tf_op jit(solution)/shard_map/while/body/eval_jaxpr/hrk,khd->hrd/dot_general | solution.py:26
  147.7 2.9 fusion.46
  152.7 4.6 %fusion.49 = f32[8,512,128]{2,1,0:T(8,128)S(1)} fusion(f32[8,512,128]{2,1,0:T(8,128)S(1)} %copy-done.5, f32[8,512,512]{2,1,0:T(8,128)S(1)} %get-tuple-element.272, f32[8,512]{1,0:T(8,128)S(1)} %select_maximum_fusion.2, pred[512,512]{0,1:T(8,128)(4,1)S(1)} %fusion.45, bf16[4096,2,8,128]{3,0,2,1:T(8,128)(2,1)} %get-tuple-element.307, ...), kind=kOutput, calls=%fused_computation.8.clone.1 | convolution fusion | flops 548929536 | bytes 13926409 | tf_op jit(solution)/shard_map/while/body/eval_jaxpr/hrk,khd->hrd/dot_general | solution.py:26
  159.4 2.9 fusion.46
  164.4 4.6 %fusion.49 = f32[8,512,128]{2,1,0:T(8,128)S(1)} fusion(f32[8,512,128]{2,1,0:T(8,128)S(1)} %copy-done.5, f32[8,512,512]{2,1,0:T(8,128)S(1)} %get-tuple-element.272, f32[8,512]{1,0:T(8,128)S(1)} %select_maximum_fusion.2, pred[512,512]{0,1:T(8,128)(4,1)S(1)} %fusion.45, bf16[4096,2,8,128]{3,0,2,1:T(8,128)(2,1)} %get-tuple-element.307, ...), kind=kOutput, calls=%fused_computation.8.clone.1 | convolution fusion | flops 548929536 | bytes 13926409 | tf_op jit(solution)/shard_map/while/body/eval_jaxpr/hrk,khd->hrd/dot_general | solution.py:26
  171.1 2.9 fusion.46
  176.1 4.6 %fusion.49 = f32[8,512,128]{2,1,0:T(8,128)S(1)} fusion(f32[8,512,128]{2,1,0:T(8,128)S(1)} %copy-done.5, f32[8,512,512]{2,1,0:T(8,128)S(1)} %get-tuple-element.272, f32[8,512]{1,0:T(8,128)S(1)} %select_maximum_fusion.2, pred[512,512]{0,1:T(8,128)(4,1)S(1)} %fusion.45, bf16[4096,2,8,128]{3,0,2,1:T(8,128)(2,1)} %get-tuple-element.307, ...), kind=kOutput, calls=%fused_computation.8.clone.1 | convolution fusion | flops 548929536 | bytes 13926409 | tf_op jit(solution)/shard_map/while/body/eval_jaxpr/hrk,khd->hrd/dot_general | solution.py:26
  182.8 2.9 fusion.46
  187.8 4.6 %fusion.49 = f32[8,512,128]{2,1,0:T(8,128)S(1)} fusion(f32[8,512,128]{2,1,0:T(8,128)S(1)} %copy-done.5, f32[8,512,512]{2,1,0:T(8,128)S(1)} %get-tuple-element.272, f32[8,512]{1,0:T(8,128)S(1)} %select_maximum_fusion.2, pred[512,512]{0,1:T(8,128)(4,1)S(1)} %fusion.45, bf16[4096,2,8,128]{3,0,2,1:T(8,128)(2,1)} %get-tuple-element.307, ...), kind=kOutput, calls=%fused_computation.8.clone.1 | convolution fusion | flops 548929536 | bytes 13926409 | tf_op jit(solution)/shard_map/while/body/eval_jaxpr/hrk,khd->hrd/dot_general | solution.py:26
  194.5 2.9 fusion.46
  197.4 2.0 fusion.47
  199.5 4.6 %fusion.49 = f32[8,512,128]{2,1,0:T(8,128)S(1)} fusion(f32[8,512,128]{2,1,0:T(8,128)S(1)} %copy-done.5, f32[8,512,512]{2,1,0:T(8,128)S(1)} %get-tuple-element.272, f32[8,512]{1,0:T(8,128)S(1)} %select_maximum_fusion.2, pred[512,512]{0,1:T(8,128)(4,1)S(1)} %fusion.45, bf16[4096,2,8,128]{3,0,2,1:T(8,128)(2,1)} %get-tuple-element.307, ...), kind=kOutput, calls=%fused_computation.8.clone.1 | convolution fusion | flops 548929536 | bytes 13926409 | tf_op jit(solution)/shard_map/while/body/eval_jaxpr/hrk,khd->hrd/dot_general | solution.py:26
  206.2 2.9 fusion.46
  211.1 4.6 %fusion.49 = f32[8,512,128]{2,1,0:T(8,128)S(1)} fusion(f32[8,512,128]{2,1,0:T(8,128)S(1)} %copy-done.5, f32[8,512,512]{2,1,0:T(8,128)S(1)} %get-tuple-element.272, f32[8,512]{1,0:T(8,128)S(1)} %select_maximum_fusion.2, pred[512,512]{0,1:T(8,128)(4,1)S(1)} %fusion.45, bf16[4096,2,8,128]{3,0,2,1:T(8,128)(2,1)} %get-tuple-element.307, ...), kind=kOutput, calls=%fused_computation.8.clone.1 | convolution fusion | flops 548929536 | bytes 13926409 | tf_op jit(solution)/shard_map/while/body/eval_jaxpr/hrk,khd->hrd/dot_general | solution.py:26
  217.1 9.1 %bitcast_convert_fusion = bf16[512,4096]{1,0:T(8,128)(2,1)} fusion(bf16[8,128,4096]{2,1,0:T(8,128)(2,1)} %param.11, f32[8,512,128]{2,1,0:T(8,128)} %get-tuple-element.145, f32[8,512]{1,0:T(8,128)S(1)} %get-tuple-element.146), kind=kOutput, calls=%fused_computation.27 | convolution fusion | flops 4298113024 | bytes 14696448 | tf_op jit(solution)/shard_map/rhd,hdo->ro/dot_general | solution.py:79
  226.3 77.8 %reduce-scatter.2.cloned.1.call-done = bf16[128,4096]{1,0:T(8,128)(2,1)} async-done(((bf16[512,4096]{1,0:T(8,128)(2,1)}), bf16[128,4096]{1,0:T(8,128)(2,1)}) %reduce-scatter.2.cloned.1.call-update) | async-done | bytes 1048592 | tf_op jit(solution)/shard_map/reduce_scatter | solution.py:78
  (100 shorter events, 37.1 us)
Async XLA Ops:
  6.5 1.0 copy-start
  6.5 117.1 %all-gather.3.cloned.1.call-start = ((), (), s32[]{:S(2)}) async-start(), calls=%async_computation.1 | async-start | bytes 18874368 | tf_op jit(solution)/shard_map/all_gather | solution.py:72
  13.1 20.4 %copy-start.3 = (s32[512]{0:T(512)S(1)}, s32[512]{0:T(512)}, u32[]{:S(2)}) copy-start(s32[512]{0:T(512)} %param.14) | copy-start | bytes 6148
  13.1 28.5 %copy-start.4 = (s32[32,32]{1,0:T(8,128)S(1)}, s32[32,32]{1,0:T(8,128)}, u32[]{:S(2)}) copy-start(s32[32,32]{1,0:T(8,128)} %param.15) | copy-start | bytes 12292
  30.2 1.6 copy-start.2
  33.4 270.7 %reduce-scatter.2.cloned.1.call-start = ((), (), s32[]{:S(2)}) async-start(), calls=%async_computation.2 | async-start | bytes 5242880 | tf_op jit(solution)/shard_map/reduce_scatter | solution.py:78
  124.3 5.0 %copy-start.5 = (f32[8,512,128]{2,1,0:T(8,128)S(1)}, f32[8,512,128]{2,1,0:T(8,128)}, u32[]{:S(2)}) copy-start(f32[8,512,128]{2,1,0:T(8,128)} %get-tuple-element.291) | copy-start | bytes 6291460 | tf_op jit(solution)/shard_map/while
  133.9 1.3 copy-start.6
  136.0 5.0 %copy-start.5 = (f32[8,512,128]{2,1,0:T(8,128)S(1)}, f32[8,512,128]{2,1,0:T(8,128)}, u32[]{:S(2)}) copy-start(f32[8,512,128]{2,1,0:T(8,128)} %get-tuple-element.291) | copy-start | bytes 6291460 | tf_op jit(solution)/shard_map/while
  145.6 1.3 copy-start.6
  147.7 5.0 %copy-start.5 = (f32[8,512,128]{2,1,0:T(8,128)S(1)}, f32[8,512,128]{2,1,0:T(8,128)}, u32[]{:S(2)}) copy-start(f32[8,512,128]{2,1,0:T(8,128)} %get-tuple-element.291) | copy-start | bytes 6291460 | tf_op jit(solution)/shard_map/while
  157.3 1.3 copy-start.6
  159.4 5.0 %copy-start.5 = (f32[8,512,128]{2,1,0:T(8,128)S(1)}, f32[8,512,128]{2,1,0:T(8,128)}, u32[]{:S(2)}) copy-start(f32[8,512,128]{2,1,0:T(8,128)} %get-tuple-element.291) | copy-start | bytes 6291460 | tf_op jit(solution)/shard_map/while
  169.0 1.3 copy-start.6
  171.1 5.0 %copy-start.5 = (f32[8,512,128]{2,1,0:T(8,128)S(1)}, f32[8,512,128]{2,1,0:T(8,128)}, u32[]{:S(2)}) copy-start(f32[8,512,128]{2,1,0:T(8,128)} %get-tuple-element.291) | copy-start | bytes 6291460 | tf_op jit(solution)/shard_map/while
  180.7 1.3 copy-start.6
  182.8 5.0 %copy-start.5 = (f32[8,512,128]{2,1,0:T(8,128)S(1)}, f32[8,512,128]{2,1,0:T(8,128)}, u32[]{:S(2)}) copy-start(f32[8,512,128]{2,1,0:T(8,128)} %get-tuple-element.291) | copy-start | bytes 6291460 | tf_op jit(solution)/shard_map/while
  192.4 1.3 copy-start.6
  194.5 5.0 %copy-start.5 = (f32[8,512,128]{2,1,0:T(8,128)S(1)}, f32[8,512,128]{2,1,0:T(8,128)}, u32[]{:S(2)}) copy-start(f32[8,512,128]{2,1,0:T(8,128)} %get-tuple-element.291) | copy-start | bytes 6291460 | tf_op jit(solution)/shard_map/while
  204.1 1.3 copy-start.6
  206.2 5.0 %copy-start.5 = (f32[8,512,128]{2,1,0:T(8,128)S(1)}, f32[8,512,128]{2,1,0:T(8,128)}, u32[]{:S(2)}) copy-start(f32[8,512,128]{2,1,0:T(8,128)} %get-tuple-element.291) | copy-start | bytes 6291460 | tf_op jit(solution)/shard_map/while
  215.8 1.3 copy-start.6
  217.1 87.0 %copy-start.1 = (f32[16,4096]{1,0:T(8,128)S(1)}, f32[16,4096]{1,0:T(8,128)}, u32[]{:S(2)}) copy-start(f32[16,4096]{1,0:T(8,128)} %param.12) | copy-start | bytes 786436
Sparse Core Ops, SparseCore 0:
  33.5 90.0 all-gather.2
  226.4 77.6 reduce-scatter.1
where the time goes:
time: 313 us; the launch traced here: 311 us
  waiting for transfers between devices  158 us (50%)
  matrix products  97.3 us (31%)
  other arithmetic  17.3 us (6%)
  local copies, waits for them, and re-layouts  16.1 us (5%)
  between operations  13.5 us (4%)
  blocking collectives  8.11 us (3%)
    all_gather x1, waiting for transfers between devices, per_device(): lax.all_gather(kv_local, 'ctx', axis=0, tiled=True)  80.1 us
    reduce_scatter x1, waiting for transfers between devices, per_device(): lax.psum_scatter(jnp.einsum('rhd,hdo->ro', attended_rows, out_weight, pre...  77.8 us
    dot_general x8, matrix products, score_block(): jnp.einsum('hrk,khd->hrd', weights.astype(jnp.bfloat16), value_rows, pref...  36.8 us
    dot_general x8, matrix products, score_block(): jnp.einsum('rhd,khd->hrk', queries, key_rows, preferred_element_type=jnp....  23 us
    dot_general x1, matrix products, per_device(): jnp.einsum('td,dchk->tchk', moduled, qkv_weight, preferred_element_type=j...  17.1 us
    reduce_sum x8, other arithmetic, score_block(): totals = totals * factor + jnp.sum(weights, axis=2)  16.3 us
    while x40, local copies, waits for them, and re-layouts  10.7 us
    dot_general x1, matrix products, per_device(): jnp.einsum('rhd,hdo->ro', attended_rows, out_weight, preferred_element_ty...  9.13 us
  transfers between devices with their start and end apart: 2, of which 2 were waited for; matrix products, arithmetic and copies ran while one was open for 1% of the time, Pallas kernels for 0%

commit v1 on v0

--- a/solution.py
+++ b/solution.py
@@ -1,8 +1,11 @@
+import functools
 import math
 
 import jax
 import jax.numpy as jnp
 from jax import lax
+from jax.experimental import pallas as pl
+from jax.experimental.pallas import tpu as pltpu
 from jax.sharding import PartitionSpec as P
 
 
@@ -85,6 +88,255 @@
     )
 
 
+def exchange(sources, targets, sends, recvs, peer):
+    return [
+        pltpu.make_async_remote_copy(
+            src_ref=source,
+            dst_ref=target,
+            send_sem=send,
+            recv_sem=recv,
+            device_id={"ctx": peer},
+            device_id_type=pl.DeviceIdType.MESH,
+        )
+        for source, target, send, recv in zip(sources, targets, sends, recvs)
+    ]
+
+
+def attend_kernel(
+    n, score_scale, qkv_ref, clip_ref, bias_ref, out_ref,
+    query_buf, key_buf, value_buf, clip_buf, score_buf, top_buf, sum_buf, done_buf,
+    send_sem, recv_sem, local_sem, back_send, back_recv, back_local,
+):
+    me = lax.axis_index("ctx")
+    rows = qkv_ref.shape[2]
+    size = qkv_ref.shape[3]
+    lanes = clip_ref.shape[1]
+
+    def span(block):
+        return pl.ds(pl.multiple_of(block * rows, rows), rows)
+
+    def landing(owner):
+        return [
+            query_buf.at[span(owner), pl.ds(0, size)],
+            key_buf.at[span(owner), pl.ds(0, size)],
+            value_buf.at[span(owner), pl.ds(0, size)],
+            clip_buf.at[owner],
+        ]
+
+    def leaving(peer):
+        return [qkv_ref.at[0, peer], qkv_ref.at[1, peer], qkv_ref.at[2, peer], clip_ref]
+
+    barrier = pltpu.get_barrier_semaphore()
+    for step in range(1, n):
+        pl.semaphore_signal(
+            barrier, inc=1, device_id={"ctx": lax.rem(me + step, n)},
+            device_id_type=pl.DeviceIdType.MESH,
+        )
+    pl.semaphore_wait(barrier, n - 1)
+
+    def outgoing(peer):
+        return exchange(
+            leaving(peer), landing(me),
+            [send_sem.at[item, peer] for item in range(4)],
+            [recv_sem.at[item, me] for item in range(4)], peer,
+        )
+
+    def incoming(owner):
+        return exchange(
+            leaving(owner), landing(owner),
+            [send_sem.at[item, owner] for item in range(4)],
+            [recv_sem.at[item, owner] for item in range(4)], owner,
+        )
+
+    def send_step(step, carry):
+        for copy in outgoing(lax.rem(me + step, n)):
+            copy.start()
+        return carry
+
+    lax.fori_loop(1, n, send_step, 0)
+    own = [
+        pltpu.make_async_copy(source, target, local_sem.at[item])
+        for item, (source, target) in enumerate(zip(leaving(me), landing(me)))
+    ]
+    for copy in own:
+        copy.start()
+    value_buf[:, size:] = jnp.ones((n * rows, size), value_buf.dtype)
+    for copy in own:
+        copy.wait()
+
+    def take(owner):
+        @pl.when(owner != me)
+        def _():
+            for copy in incoming(owner):
+                copy.wait_recv()
+
+        ids = lax.broadcasted_iota(jnp.int32, (lanes, lanes), 0)
+        for part in range(rows // lanes):
+            row = clip_buf[owner, pl.ds(part, 1), :]
+            hot = jnp.where(ids == row, 1.0, 0.0).T.astype(jnp.bfloat16)
+            at = pl.ds(pl.multiple_of(owner * rows + part * lanes, lanes), lanes)
+            key_buf[at, size:] = hot
+            query_buf[at, size:] = jnp.dot(
+                hot, bias_ref[...], preferred_element_type=jnp.float32
+            ).astype(jnp.bfloat16)
+
+    def back(block):
+        return exchange(
+            [done_buf.at[block]], [out_ref.at[me]],
+            [back_send.at[block]], [back_recv.at[me]], block,
+        )[0]
+
+    def back_in(owner):
+        return exchange(
+            [done_buf.at[owner]], [out_ref.at[owner]],
+            [back_send.at[owner]], [back_recv.at[owner]], owner,
+        )[0]
+
+    own_back = pltpu.make_async_copy(done_buf.at[me], out_ref.at[me], back_local)
+    take(0)
+
+    def one_block(block, carry):
+        @pl.when(block < n - 1)
+        def _():
+            take(block + 1)
+
+        count = jnp.minimum(block + 2, n)
+        top_buf[...] = jnp.full(top_buf.shape, -jnp.inf, jnp.float32)
+
+        def score(at, inner):
+            found = lax.dot_general(
+                query_buf[span(block), :], key_buf[span(at), :],
+                (((1,), (1,)), ((), ())), preferred_element_type=jnp.float32,
+            )
+            score_buf[at] = found
+            top = top_buf[...]
+            for part in range(rows // lanes):
+                top = jnp.maximum(top, found[:, part * lanes : (part + 1) * lanes])
+            top_buf[...] = top
+            return inner
+
+        lax.fori_loop(0, count, score, 0)
+        highest = jnp.max(top_buf[...], axis=1, keepdims=True) * score_scale
+        top_buf[...] = jnp.broadcast_to(highest, top_buf.shape)
+        sum_buf[...] = jnp.zeros(sum_buf.shape, jnp.float32)
+
+        def weigh(at, inner):
+            top = top_buf[...]
+            weights = jnp.concatenate(
+                [
+                    jnp.exp2(
+                        score_buf[at, :, part * lanes : (part + 1) * lanes] * score_scale - top
+                    ).astype(jnp.bfloat16)
+                    for part in range(rows // lanes)
+                ],
+                axis=1,
+            )
+            sum_buf[...] += jnp.dot(
+                weights, value_buf[span(at), :], preferred_element_type=jnp.float32
+            )
+            return inner
+
+        lax.fori_loop(0, count, weigh, 0)
+        done_buf[block] = (sum_buf[:, :size] / sum_buf[:, size:]).astype(jnp.bfloat16)
+
+        @pl.when(block != me)
+        def _():
+            back(block).start()
+
+        @pl.when(block == me)
+        def _():
+            own_back.start()
+
+        return carry
+
+    lax.fori_loop(0, n, one_block, 0)
+
+    def finish(step, carry):
+        peer = lax.rem(me + step, n)
+        for copy in outgoing(peer):
+            copy.wait_send()
+        back(peer).wait_send()
+        back_in(peer).wait_recv()
+        return carry
+
+    lax.fori_loop(1, n, finish, 0)
+    own_back.wait()
+
+
+def attend_heads(qkv, clip_rows, bias, n):
+    _, heads, rows, size = qkv.shape
+    lanes = clip_rows.shape[1]
+    bf16, f32 = jnp.bfloat16, jnp.float32
+    return pl.pallas_call(
+        functools.partial(attend_kernel, n, math.log2(math.e) / math.sqrt(size)),
+        out_shape=jax.ShapeDtypeStruct((heads, rows, size), bf16),
+        in_specs=[
+            pl.BlockSpec(memory_space=pltpu.VMEM),
+            pl.BlockSpec(memory_space=pltpu.VMEM),
+            pl.BlockSpec(memory_space=pltpu.VMEM),
+        ],
+        out_specs=pl.BlockSpec(memory_space=pltpu.VMEM),
+        scratch_shapes=[
+            pltpu.VMEM((n * rows, size + lanes), bf16),
+            pltpu.VMEM((n * rows, size + lanes), bf16),
+            pltpu.VMEM((n * rows, 2 * size), bf16),
+            pltpu.VMEM((n, 8, lanes), jnp.int32),
+            pltpu.VMEM((n, rows, rows), f32),
+            pltpu.VMEM((rows, lanes), f32),
+            pltpu.VMEM((rows, 2 * size), f32),
+            pltpu.VMEM((n, rows, size), bf16),
+            pltpu.SemaphoreType.DMA((4, n)),
+            pltpu.SemaphoreType.DMA((4, n)),
+            pltpu.SemaphoreType.DMA((4,)),
+            pltpu.SemaphoreType.DMA((n,)),
+            pltpu.SemaphoreType.DMA((n,)),
+            pltpu.SemaphoreType.DMA,
+        ],
+        compiler_params=pltpu.CompilerParams(
+            collective_id=0, has_side_effects=True, vmem_limit_bytes=48 * 2**20
+        ),
+        cost_estimate=pl.CostEstimate(
+            flops=5 * n * n * rows * rows * size, bytes_accessed=4 * n * rows * size * 2,
+            transcendentals=n * n * rows * rows // 2,
+        ),
+    )(qkv, clip_rows, bias)
+
+
+def modulate(activations, mod_table, clip_level, clip_of, clip_count):
+    level_count = mod_table.shape[0]
+    clip_ids = lax.broadcasted_iota(jnp.int32, (1, clip_count), 1)
+    level_ids = lax.broadcasted_iota(jnp.int32, (1, level_count), 1)
+    tok_hot = clip_of[:, None] == clip_ids
+    level_rows = jnp.sum(jnp.where(tok_hot, clip_level[None, :], 0), axis=1)
+    level_hot = (level_rows[:, None] == level_ids).astype(jnp.float32)
+    modulation = jnp.dot(level_hot, mod_table, precision=lax.Precision.HIGHEST)
+    return (activations.astype(jnp.float32) * (1.0 + modulation)).astype(jnp.bfloat16)
+
+
+def per_device_heads(
+    n, activations, qkv_weight, out_weight, mod_table, clip_level, clip_of, visible
+):
+    clip_count = visible.shape[0]
+    lanes = 128
+    moduled = modulate(activations, mod_table, clip_level, clip_of, clip_count)
+    qkv = jnp.einsum(
+        "td,dchk->chtk", moduled, qkv_weight, preferred_element_type=jnp.float32
+    ).astype(jnp.bfloat16)
+    clip_rows = clip_of.reshape(-1, lanes)
+    clip_rows = jnp.pad(clip_rows, ((0, 8 - clip_rows.shape[0]), (0, 0)))
+    bias = jnp.where(visible > 0, 0.0, -(2.0**100)).astype(jnp.bfloat16)
+    bias = jnp.pad(bias, ((0, lanes - clip_count), (0, lanes - clip_count)))
+    attended = attend_heads(qkv, clip_rows, bias, n)
+    return lax.psum_scatter(
+        jnp.einsum(
+            "htd,hdo->to", attended, out_weight, preferred_element_type=jnp.float32
+        ).astype(jnp.bfloat16),
+        "head",
+        scatter_dimension=0,
+        tiled=True,
+    )
+
+
 def solution(mesh):
     placed = (
         P("ctx", None),
@@ -95,6 +347,15 @@
         P("ctx"),
         P(),
     )
+    n = mesh.shape["ctx"]
+
+    def pick(activations, qkv_weight, out_weight, mod_table, clip_level, clip_of, visible):
+        rows, heads, size = clip_of.shape[0], qkv_weight.shape[2], qkv_weight.shape[3]
+        fits = heads == n and size == 128 and rows % 128 == 0 and 256 <= rows <= 1024
+        fits = fits and visible.shape[0] <= 128
+        body = functools.partial(per_device_heads, n) if fits else per_device
+        return body(activations, qkv_weight, out_weight, mod_table, clip_level, clip_of, visible)
+
     return jax.shard_map(
-        per_device, mesh=mesh, in_specs=placed, out_specs=P(("ctx", "head"), None), check_vma=False
-    )
+        pick, mesh=mesh, in_specs=placed, out_specs=P(("ctx", "head"), None), check_vma=False
+    )

time: 313 us -> 197 us (0.63)
  waiting for transfers between devices: 158 us -> 82.9 us
  matrix products: 97.3 us -> 29.2 us
  Pallas kernels: 0 us -> 67.6 us
  local copies, waits for them, and re-layouts: 16.1 us -> 0.04 us
  other arithmetic: 17.3 us -> 1.55 us
  blocking collectives: 8.11 us -> 0 us
    all_gather x1 -> x0, waiting for transfers between devices: 80.1 us -> none  [per_device(): lax.all_gather(kv_local, 'ctx', axis=0, tiled=True)]
    dot_general x28 -> x3, matrix products: 97.3 us -> 29.2 us  [the longest x1 17.2 us: per_device_heads(): jnp.einsum('td,dchk->chtk', moduled, qkv_weight, preferred_element_type=j...]
    pallas_call x0 -> x1, Pallas kernels: none -> 67.6 us  [attend_heads(): pl.pallas_call(functools.partial(attend_kernel, n, math.log2(math.e) / ma...]
    reduce_sum x9 -> x1, other arithmetic: 17.1 us -> 0.79 us  [modulate(): level_rows = jnp.sum(jnp.where(tok_hot, clip_level[None, :], 0), axis=1)]
    while x40 -> x0, local copies, waits for them, and re-layouts: 10.7 us -> none
    all_gather x1 -> x0, blocking collectives: 8.11 us -> none  [per_device(): lax.all_gather(clip_of, 'ctx', axis=0, tiled=True)]
    reduce_scatter x1, waiting for transfers between devices: 77.8 us -> 82.9 us  [per_device_heads(): lax.psum_scatter(jnp.einsum('htd,hdo->to', attended, out_weight, preferre...]
  transfers between devices with their start and end apart: 2 -> 1, of which waited for: 2 -> 1; matrix products, arithmetic and copies ran while one was open for 1% -> 0% of each run, Pallas kernels for 0% -> 0%
where the time goes in v1:
time: 197 us; the launch traced here: 195 us
  waiting for transfers between devices  82.9 us (42%)
  Pallas kernels  67.6 us (34%)
  matrix products  29.2 us (15%)
  between operations  13.5 us (7%)
    reduce_scatter x1, waiting for transfers between devices, per_device_heads(): lax.psum_scatter(jnp.einsum('htd,hdo->to', attended, out_weight, preferre...  82.9 us
    pallas_call x1, Pallas kernels, attend_heads(): pl.pallas_call(functools.partial(attend_kernel, n, math.log2(math.e) / ma...  67.6 us
    dot_general x1, matrix products, per_device_heads(): jnp.einsum('td,dchk->chtk', moduled, qkv_weight, preferred_element_type=j...  17.2 us
    dot_general x1, matrix products, per_device_heads(): jnp.einsum('htd,hdo->to', attended, out_weight, preferred_element_type=jn...  6.2 us
    dot_general x1, matrix products, modulate(): modulation = jnp.dot(level_hot, mod_table, precision=lax.Precision.HIGHEST)  5.74 us
  transfers between devices with their start and end apart: 1, of which 1 were waited for; matrix products, arithmetic and copies ran while one was open for 0% of the time, Pallas kernels for 0%

profile of v1, /device:TPU:14, one launch (start us, length us, event | category | flops | bytes accessed | tf_op | source)
XLA Modules:
  0.0 194.7 jit_solution(13227733495305074109)
XLA Ops:
  6.5 0.0 copy-start
  6.5 0.0 reduce-scatter.2.cloned.1.call-start
  6.5 0.8 select_convert_fusion
  7.3 0.8 select_reduce_fusion
  8.1 0.0 copy-done
  8.1 0.0 slice-start
  8.1 5.7 %fusion.2 = bf16[512,4096,1,1]{1,0,3,2:T(8,128)(2,1)S(1)} fusion(f32[16,4096]{1,0:T(8,128)S(1)} %copy-done, bf16[512,4096]{1,0:T(8,128)(2,1)} %param.7, s32[512]{0:T(512)S(1)} %select_reduce_fusion), kind=kOutput, calls=%fused_computation.4 | convolution fusion | flops 411049984 | bytes 8652800 | tf_op jit(solution)/shard_map/dot_general | solution.py:312
  13.9 0.0 copy-start.1
  13.9 0.0 slice-start.1
  13.9 17.2 %convert_bitcast_fusion.qkv_ref = bf16[3,8,512,128]{3,2,1,0:T(8,128)(2,1)S(1)} fusion(bf16[512,4096,1,1]{1,0,3,2:T(8,128)(2,1)S(1)} %fusion.2, bf16[4096,3,8,128]{3,2,1,0:T(8,128)(2,1)} %param.8), kind=kOutput, calls=%fused_computation.5 | convolution fusion | flops 12886474752 | bytes 32505856 | tf_op jit(solution)/shard_map/td,dchk->chtk/dot_general | solution.py:322
  31.1 0.0 copy-done.1
  31.1 67.6 %shard_map.73 = bf16[8,512,128]{2,1,0:T(8,128)(2,1)S(1)} custom-call(bf16[3,8,512,128]{3,2,1,0:T(8,128)(2,1)S(1)} %convert_bitcast_fusion.qkv_ref, s32[8,128]{1,0:T(8,128)S(1)} %pad.8.clip_ref, bf16[128,128]{1,0:T(8,128)(2,1)S(1)} %pad.9.bias_ref), custom_call_target="tpu_custom_call" | custom-call | flops 10737418240 | bytes 4194304 | tf_op jit(solution)/shard_map/pallas_call | solution.py:270
  98.8 0.0 slice-done
  98.8 0.0 slice-done.1
  98.8 6.2 %bitcast_convert_fusion = bf16[512,4096]{1,0:T(8,128)(2,1)} fusion(bf16[8,512,128]{2,1,0:T(8,128)(2,1)S(1)} %shard_map.73, bf16[8,128,4096]{2,1,0:T(8,128)(2,1)S(1)} %bitcast.15), kind=kOutput, calls=%fused_computation.2 | convolution fusion | flops 4297064448 | bytes 13631488 | tf_op jit(solution)/shard_map/htd,hdo->to/dot_general | solution.py:331
  105.0 0.0 reduce-scatter.2.cloned.1.call-update
  105.0 82.9 %reduce-scatter.2.cloned.1.call-done = bf16[128,4096]{1,0:T(8,128)(2,1)} async-done(((bf16[512,4096]{1,0:T(8,128)(2,1)}), bf16[128,4096]{1,0:T(8,128)(2,1)}) %reduce-scatter.2.cloned.1.call-update) | async-done | bytes 1048592 | tf_op jit(solution)/shard_map/reduce_scatter | solution.py:330
  (3 shorter events, 0.0 us)
Async XLA Ops:
  6.5 1.6 copy-start
  6.5 181.4 %reduce-scatter.2.cloned.1.call-start = ((), (), s32[]{:S(2)}) async-start(), calls=%async_computation.1 | async-start | bytes 5242880 | tf_op jit(solution)/shard_map/reduce_scatter | solution.py:330
  8.1 90.7 %slice-start = ((s8[8388608]{0:T(1024)(128)(4,1)}), s8[4194304]{0:T(1024)(128)(4,1)S(1)}, s32[]{:S(2)}) async-start(s8[8388608]{0:T(1024)(128)(4,1)} %bitcast.14), calls=%async_computation.2 | async-start | bytes 8388608
  13.9 17.3 %copy-start.1 = (s32[512]{0:T(512)S(1)}, s32[512]{0:T(512)}, u32[]{:S(2)}) copy-start(s32[512]{0:T(512)} %param.12) | copy-start | bytes 6148
  13.9 84.9 %slice-start.1 = ((s8[8388608]{0:T(1024)(128)(4,1)}), s8[4194304]{0:T(1024)(128)(4,1)S(1)}, s32[]{:S(2)}) async-start(s8[8388608]{0:T(1024)(128)(4,1)} %bitcast.14), calls=%async_computation.3 | async-start | bytes 8388608
Sparse Core Ops, SparseCore 0:
  105.2 82.6 reduce-scatter.1

commit v2 on v1

--- a/solution.py
+++ b/solution.py
@@ -302,6 +302,196 @@
     )(qkv, clip_rows, bias)
 
 
+def project_kernel(
+    pieces, attended_ref, weight_ref, out_ref,
+    part_buf, send_buf, up_buf, down_buf, send_sem, up_sem, down_sem,
+):
+    plane = lax.axis_index("head")
+    last = part_buf.shape[0] - 1
+    rows = part_buf.shape[1]
+    width = part_buf.shape[2] // pieces
+    heads, size, _ = weight_ref.shape
+    middle = (plane > 0) & (plane < last)
+
+    def columns(piece):
+        return pl.ds(pl.multiple_of(piece * width, width), width)
+
+    barrier = pltpu.get_barrier_semaphore()
+
+    @pl.when(plane > 0)
+    def _():
+        pl.semaphore_signal(
+            barrier, inc=1, device_id={"head": plane - 1}, device_id_type=pl.DeviceIdType.MESH
+        )
+
+    @pl.when(plane < last)
+    def _():
+        pl.semaphore_signal(
+            barrier, inc=1, device_id={"head": plane + 1}, device_id_type=pl.DeviceIdType.MESH
+        )
+
+    @pl.when(middle)
+    def _():
+        pl.semaphore_wait(barrier, 2)
+
+    @pl.when(jnp.logical_not(middle))
+    def _():
+        pl.semaphore_wait(barrier, 1)
+
+    def upward(share, piece, peer):
+        return pltpu.make_async_remote_copy(
+            src_ref=send_buf.at[share, :, columns(piece)],
+            dst_ref=up_buf.at[share, :, columns(piece)],
+            send_sem=send_sem.at[share, piece],
+            recv_sem=up_sem.at[share, piece],
+            device_id={"head": peer},
+            device_id_type=pl.DeviceIdType.MESH,
+        )
+
+    def downward(share, piece, peer):
+        return pltpu.make_async_remote_copy(
+            src_ref=send_buf.at[share, :, columns(piece)],
+            dst_ref=down_buf.at[share, :, columns(piece)],
+            send_sem=send_sem.at[share, piece],
+            recv_sem=down_sem.at[share, piece],
+            device_id={"head": peer},
+            device_id_type=pl.DeviceIdType.MESH,
+        )
+
+    near = jnp.where(plane == 0, 1, plane - 1)
+    low = jnp.minimum(plane, last - plane)
+
+    def compute(step, carry):
+        order, piece = step // pieces, lax.rem(step, pieces)
+        ahead = last - low
+        mirrored = jnp.where(order < ahead, last - order, order - ahead)
+        share = jnp.where(plane + plane < last, mirrored, last - mirrored)
+        at = pl.ds(pl.multiple_of(share * rows, rows), rows)
+        left = jnp.concatenate([attended_ref[head, at, :] for head in range(heads)], axis=1)
+        right = weight_ref[:, :, columns(piece)].reshape(heads * size, width)
+        part = jnp.dot(left, right, preferred_element_type=jnp.float32)
+        part_buf[share, :, columns(piece)] = part
+
+        @pl.when((plane == 0) & (share > 0))
+        def _():
+            send_buf[share, :, columns(piece)] = part.astype(jnp.bfloat16)
+            upward(share, piece, plane + 1).start()
+
+        @pl.when((plane == last) & (share < last))
+        def _():
+            send_buf[share, :, columns(piece)] = part.astype(jnp.bfloat16)
+            downward(share, piece, plane - 1).start()
+
+        return carry
+
+    lax.fori_loop(0, (last + 1) * pieces, compute, 0)
+
+    def relay_up(share, piece):
+        upward(share, piece, near).wait_recv()
+        total = part_buf[share, :, columns(piece)] + up_buf[share, :, columns(piece)].astype(
+            jnp.float32
+        )
+        send_buf[share, :, columns(piece)] = total.astype(jnp.bfloat16)
+        upward(share, piece, plane + 1).start()
+
+    def relay_down(share, piece):
+        downward(share, piece, near).wait_recv()
+        total = part_buf[share, :, columns(piece)] + down_buf[share, :, columns(piece)].astype(
+            jnp.float32
+        )
+        send_buf[share, :, columns(piece)] = total.astype(jnp.bfloat16)
+        downward(share, piece, plane - 1).start()
+
+    @pl.when(middle)
+    def _():
+        def relay(step, carry):
+            order, piece = step // pieces, lax.rem(step, pieces)
+
+            @pl.when(order < last - plane)
+            def _():
+                relay_up(last - order, piece)
+
+            @pl.when(order < plane)
+            def _():
+                relay_down(order, piece)
+
+            return carry
+
+        lax.fori_loop(0, (last - 1) * pieces, relay, 0)
+
+    def settle(piece, carry):
+        part_now = part_buf[plane, :, columns(piece)]
+
+        @pl.when(plane == 0)
+        def _():
+            downward(plane, piece, near).wait_recv()
+            total = part_now + down_buf[plane, :, columns(piece)].astype(jnp.float32)
+            out_ref[:, columns(piece)] = total.astype(jnp.bfloat16)
+
+        @pl.when(plane == last)
+        def _():
+            upward(plane, piece, near).wait_recv()
+            total = part_now + up_buf[plane, :, columns(piece)].astype(jnp.float32)
+            out_ref[:, columns(piece)] = total.astype(jnp.bfloat16)
+
+        @pl.when(middle)
+        def _():
+            upward(plane, piece, near).wait_recv()
+            downward(plane, piece, near).wait_recv()
+            total = (
+                part_now
+                + up_buf[plane, :, columns(piece)].astype(jnp.float32)
+                + down_buf[plane, :, columns(piece)].astype(jnp.float32)
+            )
+            out_ref[:, columns(piece)] = total.astype(jnp.bfloat16)
+
+        return carry
+
+    lax.fori_loop(0, pieces, settle, 0)
+
+    def finish(step, carry):
+        share, piece = step // pieces, lax.rem(step, pieces)
+
+        @pl.when(share != plane)
+        def _():
+            upward(share, piece, near).wait_send()
+
+        return carry
+
+    lax.fori_loop(0, (last + 1) * pieces, finish, 0)
+
+
+def project_heads(attended, out_weight, planes):
+    heads, rows, size = attended.shape
+    model = out_weight.shape[2]
+    share = rows // planes
+    pieces = 8
+    bf16 = jnp.bfloat16
+    return pl.pallas_call(
+        functools.partial(project_kernel, pieces),
+        out_shape=jax.ShapeDtypeStruct((share, model), bf16),
+        in_specs=[pl.BlockSpec(memory_space=pltpu.VMEM)] * 2,
+        out_specs=pl.BlockSpec(memory_space=pltpu.VMEM),
+        scratch_shapes=[
+            pltpu.VMEM((planes, share, model), jnp.float32),
+            pltpu.VMEM((planes, share, model), bf16),
+            pltpu.VMEM((planes, share, model), bf16),
+            pltpu.VMEM((planes, share, model), bf16),
+            pltpu.SemaphoreType.DMA((planes, pieces)),
+            pltpu.SemaphoreType.DMA((planes, pieces)),
+            pltpu.SemaphoreType.DMA((planes, pieces)),
+        ],
+        compiler_params=pltpu.CompilerParams(
+            collective_id=1, has_side_effects=True, vmem_limit_bytes=48 * 2**20
+        ),
+        cost_estimate=pl.CostEstimate(
+            flops=2 * rows * heads * size * model,
+            bytes_accessed=2 * heads * size * (model + rows),
+            transcendentals=0,
+        ),
+    )(attended, out_weight)
+
+
 def modulate(activations, mod_table, clip_level, clip_of, clip_count):
     level_count = mod_table.shape[0]
     clip_ids = lax.broadcasted_iota(jnp.int32, (1, clip_count), 1)
@@ -314,7 +504,7 @@
 
 
 def per_device_heads(
-    n, activations, qkv_weight, out_weight, mod_table, clip_level, clip_of, visible
+    n, planes, activations, qkv_weight, out_weight, mod_table, clip_level, clip_of, visible
 ):
     clip_count = visible.shape[0]
     lanes = 128
@@ -327,14 +517,7 @@
     bias = jnp.where(visible > 0, 0.0, -(2.0**100)).astype(jnp.bfloat16)
     bias = jnp.pad(bias, ((0, lanes - clip_count), (0, lanes - clip_count)))
     attended = attend_heads(qkv, clip_rows, bias, n)
-    return lax.psum_scatter(
-        jnp.einsum(
-            "htd,hdo->to", attended, out_weight, preferred_element_type=jnp.float32
-        ).astype(jnp.bfloat16),
-        "head",
-        scatter_dimension=0,
-        tiled=True,
-    )
+    return project_heads(attended, out_weight, planes)
 
 
 def solution(mesh):
@@ -347,13 +530,14 @@
         P("ctx"),
         P(),
     )
-    n = mesh.shape["ctx"]
+    n, planes = mesh.shape["ctx"], mesh.shape["head"]
 
     def pick(activations, qkv_weight, out_weight, mod_table, clip_level, clip_of, visible):
         rows, heads, size = clip_of.shape[0], qkv_weight.shape[2], qkv_weight.shape[3]
         fits = heads == n and size == 128 and rows % 128 == 0 and 256 <= rows <= 1024
-        fits = fits and visible.shape[0] <= 128
-        body = functools.partial(per_device_heads, n) if fits else per_device
+        fits = fits and visible.shape[0] <= 128 and planes == 4
+        fits = fits and out_weight.shape[2] % 1024 == 0
+        body = functools.partial(per_device_heads, n, planes) if fits else per_device
         return body(activations, qkv_weight, out_weight, mod_table, clip_level, clip_of, visible)
 
     return jax.shard_map(

time: 197 us -> 196 us (level)
  Pallas kernels: 67.6 us -> 171 us
  waiting for transfers between devices: 82.9 us -> 0 us
  between operations: 13.5 us -> 0.09 us
  matrix products: 29.2 us -> 22.7 us
    pallas_call x0 -> x1, Pallas kernels: none -> 103 us  [project_heads(): pl.pallas_call(functools.partial(project_kernel, pieces), out_shape=jax.S...]
    reduce_scatter x1 -> x0, waiting for transfers between devices: 82.9 us -> none  [per_device_heads(): lax.psum_scatter(jnp.einsum('htd,hdo->to', attended, out_weight, preferre...]
    dot_general x1 -> x0, matrix products: 6.2 us -> none  [per_device_heads(): jnp.einsum('htd,hdo->to', attended, out_weight, preferred_element_type=jn...]
  transfers between devices with their start and end apart: 1 -> 0, of which waited for: 1 -> 0; matrix products, arithmetic and copies ran while one was open for 0% -> 0% of each run, Pallas kernels for 0% -> 0%
where the time goes in v2:
time: 196 us
  Pallas kernels  171 us (87%)
  matrix products  22.7 us (12%)
    pallas_call x1, Pallas kernels, project_heads(): pl.pallas_call(functools.partial(project_kernel, pieces), out_shape=jax.S...  103 us
    pallas_call x1, Pallas kernels, attend_heads(): pl.pallas_call(functools.partial(attend_kernel, n, math.log2(math.e) / ma...  67.6 us
    dot_general x1, matrix products, per_device_heads(): jnp.einsum('td,dchk->chtk', moduled, qkv_weight, preferred_element_type=j...  17.1 us
    dot_general x1, matrix products, modulate(): modulation = jnp.dot(level_hot, mod_table, precision=lax.Precision.HIGHEST)  5.58 us

profile of v2, /device:TPU:14, one launch (start us, length us, event | category | flops | bytes accessed | tf_op | source)
XLA Modules:
  0.0 195.6 jit_solution(12725833599010184900)
XLA Ops:
  0.0 0.0 copy-start
  0.0 0.8 select_reduce_fusion
  0.8 0.1 copy-done
  1.0 5.6 %fusion.2 = bf16[512,4096,1,1]{1,0,3,2:T(8,128)(2,1)S(1)} fusion(f32[16,4096]{1,0:T(8,128)S(1)} %copy-done, bf16[512,4096]{1,0:T(8,128)(2,1)} %param.7, s32[512]{0:T(512)S(1)} %select_reduce_fusion), kind=kOutput, calls=%fused_computation.3 | convolution fusion | flops 411049984 | bytes 8652800 | tf_op jit(solution)/shard_map/dot_general | solution.py:502
  6.6 0.0 copy-start.1
  6.6 0.0 copy-start.2
  6.6 17.1 %convert_bitcast_fusion.qkv_ref = bf16[3,8,512,128]{3,2,1,0:T(8,128)(2,1)S(1)} fusion(bf16[512,4096,1,1]{1,0,3,2:T(8,128)(2,1)S(1)} %fusion.2, bf16[4096,3,8,128]{3,2,1,0:T(8,128)(2,1)} %param.8), kind=kOutput, calls=%fused_computation.4 | convolution fusion | flops 12886474752 | bytes 32505856 | tf_op jit(solution)/shard_map/td,dchk->chtk/dot_general | solution.py:512
  23.7 0.0 copy-done.1
  23.7 0.0 copy-done.2
  23.7 67.6 %shard_map.73.attended_ref = bf16[8,512,128]{2,1,0:T(8,128)(2,1)S(1)} custom-call(bf16[3,8,512,128]{3,2,1,0:T(8,128)(2,1)S(1)} %convert_bitcast_fusion.qkv_ref, s32[8,128]{1,0:T(8,128)S(1)} %pad.8.clip_ref, bf16[128,128]{1,0:T(8,128)(2,1)S(1)} %pad.9.bias_ref), custom_call_target="tpu_custom_call" | custom-call | flops 10737418240 | bytes 4194304 | tf_op jit(solution)/shard_map/pallas_call | solution.py:270
  91.4 103.3 %shard_map.74 = bf16[128,4096]{1,0:T(8,128)(2,1)S(1)} custom-call(bf16[8,512,128]{2,1,0:T(8,128)(2,1)S(1)} %shard_map.73.attended_ref, bf16[8,128,4096]{2,1,0:T(8,128)(2,1)} %weight_ref.1), custom_call_target="tpu_custom_call" | custom-call | flops 4294967296 | bytes 9437184 | tf_op jit(solution)/shard_map/pallas_call | solution.py:470
  194.7 1.0 copy.16
  (3 shorter events, 0.0 us)
Async XLA Ops:
  0.0 1.0 copy-start
  6.6 17.1 %copy-start.1 = (s32[32,32]{1,0:T(8,128)S(1)}, s32[32,32]{1,0:T(8,128)}, u32[]{:S(2)}) copy-start(s32[32,32]{1,0:T(8,128)} %param.13) | copy-start | bytes 12292
  6.6 17.1 %copy-start.2 = (s32[512]{0:T(512)S(1)}, s32[512]{0:T(512)}, u32[]{:S(2)}) copy-start(s32[512]{0:T(512)} %param.12) | copy-start | bytes 6148

commit v3 on v1

--- a/solution.py
+++ b/solution.py
@@ -103,14 +103,19 @@
 
 
 def attend_kernel(
-    n, score_scale, qkv_ref, clip_ref, bias_ref, out_ref,
-    query_buf, key_buf, value_buf, clip_buf, score_buf, top_buf, sum_buf, done_buf,
-    send_sem, recv_sem, local_sem, back_send, back_recv, back_local,
+    n, score_scale, planes, half, *refs
 ):
+    if half == 0:
+        qkv_ref, clip_ref, bias_ref, out_ref, query_buf, key_buf, value_buf, *scratch = refs
+        clip_buf, send_sem, recv_sem, local_sem, *scratch = scratch
+    else:
+        query_buf, key_buf, value_buf, out_ref, *scratch = refs
+    score_buf, top_buf, sum_buf, done_buf, back_send, back_recv, back_local = scratch
     me = lax.axis_index("ctx")
-    rows = qkv_ref.shape[2]
-    size = qkv_ref.shape[3]
-    lanes = clip_ref.shape[1]
+    rows = query_buf.shape[0] // n
+    size = value_buf.shape[1] // 2
+    lanes = top_buf.shape[1]
+    group = rows // planes
 
     def span(block):
         return pl.ds(pl.multiple_of(block * rows, rows), rows)
@@ -153,16 +158,17 @@
             copy.start()
         return carry
 
-    lax.fori_loop(1, n, send_step, 0)
-    own = [
-        pltpu.make_async_copy(source, target, local_sem.at[item])
-        for item, (source, target) in enumerate(zip(leaving(me), landing(me)))
-    ]
-    for copy in own:
-        copy.start()
-    value_buf[:, size:] = jnp.ones((n * rows, size), value_buf.dtype)
-    for copy in own:
-        copy.wait()
+    if half == 0:
+        lax.fori_loop(1, n, send_step, 0)
+        own = [
+            pltpu.make_async_copy(source, target, local_sem.at[item])
+            for item, (source, target) in enumerate(zip(leaving(me), landing(me)))
+        ]
+        for copy in own:
+            copy.start()
+        value_buf[:, size:] = jnp.ones((n * rows, size), value_buf.dtype)
+        for copy in own:
+            copy.wait()
 
     def take(owner):
         @pl.when(owner != me)
@@ -193,19 +199,29 @@
         )[0]
 
     own_back = pltpu.make_async_copy(done_buf.at[me], out_ref.at[me], back_local)
-    take(0)
+    if half == 0:
+        take(0)
 
     def one_block(block, carry):
-        @pl.when(block < n - 1)
-        def _():
-            take(block + 1)
+        if half == 0:
+            @pl.when(block < n - 1)
+            def _():
+                take(block + 1)
+
+        starts = [
+            pl.multiple_of(block * rows + plane * group + half * (group // 2), group // 2)
+            for plane in range(planes)
+        ]
+        mine = jnp.concatenate(
+            [query_buf[pl.ds(start, group // 2), :] for start in starts], axis=0
+        )
 
         count = jnp.minimum(block + 2, n)
         top_buf[...] = jnp.full(top_buf.shape, -jnp.inf, jnp.float32)
 
         def score(at, inner):
             found = lax.dot_general(
-                query_buf[span(block), :], key_buf[span(at), :],
+                mine, key_buf[span(at), :],
                 (((1,), (1,)), ((), ())), preferred_element_type=jnp.float32,
             )
             score_buf[at] = found
@@ -253,8 +269,9 @@
 
     def finish(step, carry):
         peer = lax.rem(me + step, n)
-        for copy in outgoing(peer):
-            copy.wait_send()
+        if half == 0:
+            for copy in outgoing(peer):
+                copy.wait_send()
         back(peer).wait_send()
         back_in(peer).wait_recv()
         return carry
@@ -263,43 +280,41 @@
     own_back.wait()
 
 
-def attend_heads(qkv, clip_rows, bias, n):
-    _, heads, rows, size = qkv.shape
-    lanes = clip_rows.shape[1]
+def attend_half(operands, n, planes, half, rows, size):
+    lanes, few = 128, rows // 2
     bf16, f32 = jnp.bfloat16, jnp.float32
+    held = [jax.ShapeDtypeStruct((n * rows, 2 * size), bf16)] * 3
+    outs = [jax.ShapeDtypeStruct((n, few, size), bf16)] + (held if half == 0 else [])
+    exchanged = [
+        pltpu.VMEM((n, 8, lanes), jnp.int32),
+        pltpu.SemaphoreType.DMA((4, n)),
+        pltpu.SemaphoreType.DMA((4, n)),
+        pltpu.SemaphoreType.DMA((4,)),
+    ]
+    scale = math.log2(math.e) / math.sqrt(size)
     return pl.pallas_call(
-        functools.partial(attend_kernel, n, math.log2(math.e) / math.sqrt(size)),
-        out_shape=jax.ShapeDtypeStruct((heads, rows, size), bf16),
-        in_specs=[
-            pl.BlockSpec(memory_space=pltpu.VMEM),
-            pl.BlockSpec(memory_space=pltpu.VMEM),
-            pl.BlockSpec(memory_space=pltpu.VMEM),
-        ],
-        out_specs=pl.BlockSpec(memory_space=pltpu.VMEM),
-        scratch_shapes=[
-            pltpu.VMEM((n * rows, size + lanes), bf16),
-            pltpu.VMEM((n * rows, size + lanes), bf16),
-            pltpu.VMEM((n * rows, 2 * size), bf16),
-            pltpu.VMEM((n, 8, lanes), jnp.int32),
-            pltpu.VMEM((n, rows, rows), f32),
-            pltpu.VMEM((rows, lanes), f32),
-            pltpu.VMEM((rows, 2 * size), f32),
-            pltpu.VMEM((n, rows, size), bf16),
-            pltpu.SemaphoreType.DMA((4, n)),
-            pltpu.SemaphoreType.DMA((4, n)),
-            pltpu.SemaphoreType.DMA((4,)),
+        functools.partial(attend_kernel, n, scale, planes, half),
+        out_shape=outs,
+        in_specs=[pl.BlockSpec(memory_space=pltpu.VMEM)] * len(operands),
+        out_specs=[pl.BlockSpec(memory_space=pltpu.VMEM)] * len(outs),
+        scratch_shapes=(exchanged if half == 0 else [])
+        + [
+            pltpu.VMEM((n, few, rows), f32),
+            pltpu.VMEM((few, lanes), f32),
+            pltpu.VMEM((few, 2 * size), f32),
+            pltpu.VMEM((n, few, size), bf16),
             pltpu.SemaphoreType.DMA((n,)),
             pltpu.SemaphoreType.DMA((n,)),
             pltpu.SemaphoreType.DMA,
         ],
         compiler_params=pltpu.CompilerParams(
-            collective_id=0, has_side_effects=True, vmem_limit_bytes=48 * 2**20
+            collective_id=half, has_side_effects=True, vmem_limit_bytes=40 * 2**20
         ),
         cost_estimate=pl.CostEstimate(
-            flops=5 * n * n * rows * rows * size, bytes_accessed=4 * n * rows * size * 2,
-            transcendentals=n * n * rows * rows // 2,
+            flops=3 * n * n * rows * rows * size, bytes_accessed=4 * n * rows * size * 2,
+            transcendentals=n * n * rows * rows // 4,
         ),
-    )(qkv, clip_rows, bias)
+    )(*operands)
 
 
 def modulate(activations, mod_table, clip_level, clip_of, clip_count):
@@ -314,7 +329,7 @@
 
 
 def per_device_heads(
-    n, activations, qkv_weight, out_weight, mod_table, clip_level, clip_of, visible
+    n, planes, activations, qkv_weight, out_weight, mod_table, clip_level, clip_of, visible
 ):
     clip_count = visible.shape[0]
     lanes = 128
@@ -326,15 +341,19 @@
     clip_rows = jnp.pad(clip_rows, ((0, 8 - clip_rows.shape[0]), (0, 0)))
     bias = jnp.where(visible > 0, 0.0, -(2.0**100)).astype(jnp.bfloat16)
     bias = jnp.pad(bias, ((0, lanes - clip_count), (0, lanes - clip_count)))
-    attended = attend_heads(qkv, clip_rows, bias, n)
-    return lax.psum_scatter(
-        jnp.einsum(
+    rows, size = qkv.shape[2:]
+
+    def project(attended):
+        return jnp.einsum(
             "htd,hdo->to", attended, out_weight, preferred_element_type=jnp.float32
-        ).astype(jnp.bfloat16),
-        "head",
-        scatter_dimension=0,
-        tiled=True,
-    )
+        ).astype(jnp.bfloat16)
+
+    attended, *held = attend_half([qkv, clip_rows, bias], n, planes, 0, rows, size)
+    held, first = lax.optimization_barrier((held, project(attended)))
+    first = lax.psum_scatter(first, "head", scatter_dimension=0, tiled=True)
+    (attended,) = attend_half(held, n, planes, 1, rows, size)
+    second = lax.psum_scatter(project(attended), "head", scatter_dimension=0, tiled=True)
+    return jnp.concatenate([first, second], axis=0)
 
 
 def solution(mesh):
@@ -347,13 +366,13 @@
         P("ctx"),
         P(),
     )
-    n = mesh.shape["ctx"]
+    n, planes = mesh.shape["ctx"], mesh.shape["head"]
 
     def pick(activations, qkv_weight, out_weight, mod_table, clip_level, clip_of, visible):
         rows, heads, size = clip_of.shape[0], qkv_weight.shape[2], qkv_weight.shape[3]
         fits = heads == n and size == 128 and rows % 128 == 0 and 256 <= rows <= 1024
-        fits = fits and visible.shape[0] <= 128
-        body = functools.partial(per_device_heads, n) if fits else per_device
+        fits = fits and visible.shape[0] <= 128 and rows % (32 * planes) == 0
+        body = functools.partial(per_device_heads, n, planes) if fits else per_device
         return body(activations, qkv_weight, out_weight, mod_table, clip_level, clip_of, visible)
 
     return jax.shard_map(

time: 197 us -> 205 us (1.041)
  the two profiles are of different devices: /device:TPU:14 before, /device:TPU:0 now
where the time goes in v3:
time: 205 us
  Pallas kernels  94.5 us (46%)
  waiting for transfers between devices  53.1 us (26%)
  matrix products  33.4 us (16%)
  between operations  13.5 us (7%)
  local copies, waits for them, and re-layouts  6.52 us (3%)
  other arithmetic  3.81 us (2%)
    pallas_call x2, Pallas kernels, attend_half(): pl.pallas_call(functools.partial(attend_kernel, n, scale, planes, half),...  94.5 us
    reduce_scatter x1, waiting for transfers between devices, per_device_heads(): lax.psum_scatter(project(attended), 'head', scatter_dimension=0, tiled=True)  45.7 us
    dot_general x1, matrix products, per_device_heads(): jnp.einsum('td,dchk->chtk', moduled, qkv_weight, preferred_element_type=j...  17.2 us
    dot_general x2, matrix products, project(): jnp.einsum('htd,hdo->to', attended, out_weight, preferred_element_type=jn...  10.5 us
    reduce_scatter x1, waiting for transfers between devices, per_device_heads(): first = lax.psum_scatter(first, 'head', scatter_dimension=0, tiled=True)  7.37 us
    unnamed x14, local copies, waits for them, and re-layouts  5.82 us
    dot_general x1, matrix products, modulate(): modulation = jnp.dot(level_hot, mod_table, precision=lax.Precision.HIGHEST)  5.73 us
  transfers between devices with their start and end apart: 2, of which 2 were waited for; matrix products, arithmetic and copies ran while one was open for 3% of the time, Pallas kernels for 18%

profile of v3, /device:TPU:0, one launch (start us, length us, event | category | flops | bytes accessed | tf_op | source)
XLA Modules:
  0.0 204.9 jit_solution(997728636232484219)
XLA Ops:
  6.5 0.0 copy-start
  6.5 0.8 select_convert_fusion
  7.3 0.8 select_reduce_fusion
  8.1 0.7 pad.8.refs_1_
  8.8 0.0 slice-start
  8.8 5.7 %fusion.2 = bf16[512,4096,1,1]{1,0,3,2:T(8,128)(2,1)S(1)} fusion(f32[16,4096]{1,0:T(8,128)S(1)} %copy-done, bf16[512,4096]{1,0:T(8,128)(2,1)} %param.7, s32[512]{0:T(512)S(1)} %select_reduce_fusion), kind=kOutput, calls=%fused_computation.5 | convolution fusion | flops 411049984 | bytes 8652800 | tf_op jit(solution)/shard_map/dot_general | solution.py:327
  14.6 0.0 slice-start.1
  14.6 17.2 %convert_bitcast_fusion.refs_0_ = bf16[3,8,512,128]{3,2,1,0:T(8,128)(2,1)S(1)} fusion(bf16[512,4096,1,1]{1,0,3,2:T(8,128)(2,1)S(1)} %fusion.2, bf16[4096,3,8,128]{3,2,1,0:T(8,128)(2,1)} %param.8), kind=kOutput, calls=%fused_computation.8 | convolution fusion | flops 12886474752 | bytes 32505856 | tf_op jit(solution)/shard_map/td,dchk->chtk/dot_general | solution.py:337
  31.8 57.7 %shard_map.73 = (bf16[8,256,128]{2,1,0:T(8,128)(2,1)S(1)}, bf16[4096,256]{1,0:T(8,128)(2,1)S(1)}, bf16[4096,256]{1,0:T(8,128)(2,1)S(1)}, bf16[4096,256]{1,0:T(8,128)(2,1)S(1)}) custom-call(bf16[3,8,512,128]{3,2,1,0:T(8,128)(2,1)S(1)} %convert_bitcast_fusion.refs_0_, s32[8,128]{1,0:T(8,128)S(1)} %pad.8.refs_1_, bf16[128,128]{1,0:T(8,128)(2,1)S(1)} %pad.9.refs_2_), custom_call_target="tpu_custom_call" | custom-call | flops 6442450944 | bytes 4194304 | tf_op jit(solution)/shard_map/pallas_call | solution.py:295
  89.5 0.0 copy-start.1
  89.5 1.3 copy-done.1
  90.8 1.3 copy-done.3
  92.1 0.0 slice-done.1
  92.1 3.5 %fusion.3 = bf16[256,4096]{1,0:T(8,128)(2,1)} fusion(bf16[8,256,128]{2,1,0:T(8,128)(2,1)S(1)} %get-tuple-element.16, bf16[8,128,4096]{2,1,0:T(8,128)(2,1)S(1)} %bitcast.23), kind=kOutput, calls=%fused_computation.6 | convolution fusion | flops 2148532224 | bytes 11010048 | tf_op jit(solution)/shard_map/htd,hdo->to/dot_general | solution.py:347
  95.7 0.0 reduce-scatter.3.cloned.1.call-update
  95.7 0.0 reduce-scatter.5.cloned.1.call-start
  95.7 1.6 copy-done.2
  97.3 1.6 copy-done.4
  98.9 36.8 %shard_map.74 = bf16[8,256,128]{2,1,0:T(8,128)(2,1)S(1)} custom-call(bf16[4096,256]{1,0:T(8,128)(2,1)S(1)} %get-tuple-element.18.refs_0_, bf16[4096,256]{1,0:T(8,128)(2,1)S(1)} %copy-done.2, bf16[4096,256]{1,0:T(8,128)(2,1)S(1)} %copy-done.4), custom_call_target="tpu_custom_call" | custom-call | flops 6442450944 | bytes 4194304 | tf_op jit(solution)/shard_map/pallas_call | solution.py:295
  135.7 6.9 %fusion.4 = bf16[256,4096]{1,0:T(8,128)(2,1)} fusion(bf16[8,256,128]{2,1,0:T(8,128)(2,1)S(1)} %shard_map.74, bf16[8,128,4096]{2,1,0:T(8,128)(2,1)} %param.9), kind=kOutput, calls=%fused_computation.7 | convolution fusion | flops 2148532224 | bytes 11010048 | tf_op jit(solution)/shard_map/htd,hdo->to/dot_general | solution.py:347
  142.7 0.0 reduce-scatter.5.cloned.1.call-update
  142.7 7.4 %reduce-scatter.3.cloned.1.call-done = bf16[64,4096]{1,0:T(8,128)(2,1)} async-done(((bf16[256,4096]{1,0:T(8,128)(2,1)}), bf16[64,4096]{1,0:T(8,128)(2,1)}) %reduce-scatter.3.cloned.1.call-update) | async-done | bytes 524304 | tf_op jit(solution)/shard_map/reduce_scatter | solution.py:353
  150.1 45.7 %reduce-scatter.5.cloned.1.call-done = bf16[64,4096]{1,0:T(8,128)(2,1)} async-done(((bf16[256,4096]{1,0:T(8,128)(2,1)}), bf16[64,4096]{1,0:T(8,128)(2,1)}) %reduce-scatter.5.cloned.1.call-update) | async-done | bytes 524304 | tf_op jit(solution)/shard_map/reduce_scatter | solution.py:355
  195.8 2.3 %pad_maximum_fusion = bf16[128,4096]{1,0:T(8,128)(2,1)} fusion(bf16[64,4096]{1,0:T(8,128)(2,1)} %reduce-scatter.5.cloned.1.call-done, bf16[64,4096]{1,0:T(8,128)(2,1)} %reduce-scatter.3.cloned.1.call-done), kind=kLoop, calls=%fused_computation.9 | loop fusion | flops 2097152 | bytes 2097152 | tf_op jit(solution)/shard_map/concatenate | solution.py:356
  (8 shorter events, 0.0 us)
Async XLA Ops:
  6.5 2.3 %copy-start = (f32[16,4096]{1,0:T(8,128)S(1)}, f32[16,4096]{1,0:T(8,128)}, u32[]{:S(2)}) copy-start(f32[16,4096]{1,0:T(8,128)} %param.10) | copy-start | bytes 786436
  6.5 143.5 %reduce-scatter.3.cloned.1.call-start = ((), (), s32[]{:S(2)}) async-start(), calls=%async_computation.2 | async-start | bytes 2621440 | tf_op jit(solution)/shard_map/reduce_scatter | solution.py:353
  8.8 83.3 %slice-start = ((s8[8388608]{0:T(1024)(128)(4,1)}), s8[4194304]{0:T(1024)(128)(4,1)S(1)}, s32[]{:S(2)}) async-start(s8[8388608]{0:T(1024)(128)(4,1)} %bitcast.22), calls=%async_computation.4 | async-start | bytes 8388608
  14.6 77.6 %slice-start.1 = ((s8[8388608]{0:T(1024)(128)(4,1)}), s8[4194304]{0:T(1024)(128)(4,1)S(1)}, s32[]{:S(2)}) async-start(s8[8388608]{0:T(1024)(128)(4,1)} %bitcast.22), calls=%async_computation.5 | async-start | bytes 8388608
  89.5 1.3 copy-start.1
  90.8 1.3 copy-start.3
  95.7 100.1 %reduce-scatter.5.cloned.1.call-start = ((), (), s32[]{:S(2)}) async-start(), calls=%async_computation.3 | async-start | bytes 2621440 | tf_op jit(solution)/shard_map/reduce_scatter | solution.py:355
  95.7 1.6 copy-start.2
  97.3 1.6 copy-start.4
Sparse Core Ops, SparseCore 0:
  95.8 54.2 reduce-scatter.2
  152.5 43.2 reduce-scatter.4

commit v4 on v2

--- a/solution.py
+++ b/solution.py
@@ -465,7 +465,7 @@
     heads, rows, size = attended.shape
     model = out_weight.shape[2]
     share = rows // planes
-    pieces = 8
+    pieces = 4
     bf16 = jnp.bfloat16
     return pl.pallas_call(
         functools.partial(project_kernel, pieces),

time: 196 us -> 179 us (0.913)
  Pallas kernels: 171 us -> 153 us
    pallas_call x1, Pallas kernels: 103 us -> 85.3 us  [project_heads(): pl.pallas_call(functools.partial(project_kernel, pieces), out_shape=jax.S...]
where the time goes in v4:
time: 179 us; the launch traced here: 178 us
  Pallas kernels  153 us (85%)
  matrix products  22.7 us (13%)
    pallas_call x1, Pallas kernels, project_heads(): pl.pallas_call(functools.partial(project_kernel, pieces), out_shape=jax.S...  85.3 us
    pallas_call x1, Pallas kernels, attend_heads(): pl.pallas_call(functools.partial(attend_kernel, n, math.log2(math.e) / ma...  67.6 us
    dot_general x1, matrix products, per_device_heads(): jnp.einsum('td,dchk->chtk', moduled, qkv_weight, preferred_element_type=j...  17.1 us
    dot_general x1, matrix products, modulate(): modulation = jnp.dot(level_hot, mod_table, precision=lax.Precision.HIGHEST)  5.58 us

profile of v4, /device:TPU:14, one launch (start us, length us, event | category | flops | bytes accessed | tf_op | source)
XLA Modules:
  0.0 177.7 jit_solution(16453344203354220012)
XLA Ops:
  0.0 0.0 copy-start
  0.0 0.8 select_reduce_fusion
  0.8 0.1 copy-done
  1.0 5.6 %fusion.2 = bf16[512,4096,1,1]{1,0,3,2:T(8,128)(2,1)S(1)} fusion(f32[16,4096]{1,0:T(8,128)S(1)} %copy-done, bf16[512,4096]{1,0:T(8,128)(2,1)} %param.7, s32[512]{0:T(512)S(1)} %select_reduce_fusion), kind=kOutput, calls=%fused_computation.3 | convolution fusion | flops 411049984 | bytes 8652800 | tf_op jit(solution)/shard_map/dot_general | solution.py:502
  6.6 0.0 copy-start.1
  6.6 0.0 copy-start.2
  6.6 17.1 %convert_bitcast_fusion.qkv_ref = bf16[3,8,512,128]{3,2,1,0:T(8,128)(2,1)S(1)} fusion(bf16[512,4096,1,1]{1,0,3,2:T(8,128)(2,1)S(1)} %fusion.2, bf16[4096,3,8,128]{3,2,1,0:T(8,128)(2,1)} %param.8), kind=kOutput, calls=%fused_computation.4 | convolution fusion | flops 12886474752 | bytes 32505856 | tf_op jit(solution)/shard_map/td,dchk->chtk/dot_general | solution.py:512
  23.7 0.0 copy-done.1
  23.7 0.0 copy-done.2
  23.7 67.6 %shard_map.73.attended_ref = bf16[8,512,128]{2,1,0:T(8,128)(2,1)S(1)} custom-call(bf16[3,8,512,128]{3,2,1,0:T(8,128)(2,1)S(1)} %convert_bitcast_fusion.qkv_ref, s32[8,128]{1,0:T(8,128)S(1)} %pad.8.clip_ref, bf16[128,128]{1,0:T(8,128)(2,1)S(1)} %pad.9.bias_ref), custom_call_target="tpu_custom_call" | custom-call | flops 10737418240 | bytes 4194304 | tf_op jit(solution)/shard_map/pallas_call | solution.py:270
  91.4 85.3 %shard_map.74 = bf16[128,4096]{1,0:T(8,128)(2,1)S(1)} custom-call(bf16[8,512,128]{2,1,0:T(8,128)(2,1)S(1)} %shard_map.73.attended_ref, bf16[8,128,4096]{2,1,0:T(8,128)(2,1)} %weight_ref.1), custom_call_target="tpu_custom_call" | custom-call | flops 4294967296 | bytes 9437184 | tf_op jit(solution)/shard_map/pallas_call | solution.py:470
  176.7 1.0 copy.16
  (3 shorter events, 0.0 us)
Async XLA Ops:
  0.0 1.0 copy-start
  6.6 17.1 %copy-start.1 = (s32[32,32]{1,0:T(8,128)S(1)}, s32[32,32]{1,0:T(8,128)}, u32[]{:S(2)}) copy-start(s32[32,32]{1,0:T(8,128)} %param.13) | copy-start | bytes 12292
  6.6 17.1 %copy-start.2 = (s32[512]{0:T(512)S(1)}, s32[512]{0:T(512)}, u32[]{:S(2)}) copy-start(s32[512]{0:T(512)} %param.12) | copy-start | bytes 6148
